TPU v7x, 256 devices: a whole 4x4x8 slice. The times are simulated.
256 devices in a mesh: front: 64 (over x, y, z_lo, core), blk: 4 (over z_hi).
Axes of the slice: x: 4, y: 4, z: 8 (z_hi: 4, z_lo: 2; z = z_hi * 2 + z_lo), core: 2. Of those that a mesh axis runs over, the one named last changes fastest.
Arguments:
- child_diag: float32 [65536, 1024], P(('front', 'blk')), as said below
- child_top: float32 [32768, 1024], P(('front', 'blk')), may hold values from -0.078125 to 0.078125
- child_rows: float32 [131072, 1024], P(('front', 'blk')), may hold values from -12 to 12
- row_owner: int32 [64, 16, 1], P('front'), may hold values from 0 to 63; in each aligned block of 16 rows (0 to 15, 16 to 31, ..., all dimensions but the last counted through in order) at most 2 rows name the same one
- row_slot: int32 [64, 16], P('front'), may hold values from 0 to 3
- col_block: int32 [64, 4], P('front'), may hold values from 0 to 1
- parent_diag: float32 [1024, 1024], P('blk'), as said below
- parent_rows: float32 [32768, 1024], P('front', 'blk'), may hold values from -6 to 6
Outputs:
- parent_factor: float32 [1024, 1024], P('blk')
- parent_panel: float32 [32768, 1024], P(('front', 'blk'))
Inputs may be any that keep to these rules, and one draw needn't show every extreme that they name: `row_owner`: within the 16 row blocks of one child no owner is named more than 2 times, and in some children one owner is named exactly 2 times. `child_diag`: each 1024 x 1024 block is symmetric with all eigenvalues at least 1. `parent_diag`: symmetric with all eigenvalues at least 24; parent_diag - diag_update has all eigenvalues at least 12.
All inputs are finite; a program needn't handle non-finite values.
Results may differ from a plain program's by a relative error of at most 0.0001.
Values sent between devices are 32-bit elements; how exact they have to be, the bound alone decides.
A program may use at most 192 MiB of HBM per device.

v0:
```python
import jax
import jax.numpy as jnp
from jax import lax
from jax.sharding import PartitionSpec as P

W = 1024
TILE = 128
TA = 4
PB = 4
HIGHEST = lax.Precision.HIGHEST


def right_solve(factor, matrix):
    return jax.scipy.linalg.solve_triangular(factor, matrix.T, lower=True).T


def blocked_cholesky(matrix):
    order_size = matrix.shape[0]
    stride = min(256, order_size)
    remaining = matrix
    factor = jnp.zeros_like(matrix)
    for offset in range(0, order_size, stride):
        finish = offset + stride
        diag_piece = jnp.linalg.cholesky(remaining[offset:finish, offset:finish])
        factor = factor.at[offset:finish, offset:finish].set(diag_piece)
        if finish < order_size:
            lower_part = right_solve(diag_piece, remaining[finish:, offset:finish])
            factor = factor.at[finish:, offset:finish].set(lower_part)
            trailing = remaining[finish:, finish:] - jnp.dot(
                lower_part, lower_part.T, precision=HIGHEST
            )
            remaining = remaining.at[finish:, finish:].set(trailing)
    return factor


def shards(
    child_diag, child_top, child_rows, row_owner, row_slot, col_block, parent_diag, parent_rows
):
    block_count = lax.axis_size("blk")
    front_count = lax.axis_size("front")
    my_block = lax.axis_index("blk")
    quarter = W // (TILE * block_count)
    block_width = W // TILE
    capacity = max(2, 8 * TA // front_count)
    diag_whole, top_whole = (
        lax.all_gather(child_diag, "blk", axis=0, tiled=True),
        lax.all_gather(child_top, "blk", axis=0, tiled=True),
    )
    factor = blocked_cholesky(diag_whole)
    top_solved = right_solve(factor, top_whole)
    rows_solved = right_solve(factor, child_rows)
    top_tiles = top_solved.reshape(block_count, TILE, W)
    schur_tiles = jnp.einsum("rw,kcw->krc", rows_solved, top_tiles, precision=HIGHEST)
    arrived = lax.all_to_all(schur_tiles, "blk", split_axis=0, concat_axis=0, tiled=True)
    arrived = arrived.reshape(block_count * TA, TILE, TILE)
    owners = row_owner[0, :, 0]
    slot_index = row_slot[0]
    column_picks = col_block[0]
    sequence = jnp.arange(owners.shape[0], dtype=jnp.int32)
    earlier = (owners[:, None] == owners[None, :]) & (sequence[None, :] < sequence[:, None])
    arrival_rank = jnp.sum(earlier.astype(jnp.int32), axis=1)
    position = owners * capacity + arrival_rank
    block_ids = jnp.arange(block_count, dtype=jnp.int32)
    my_pick = jnp.sum(jnp.where(block_ids == my_block, column_picks, 0))
    landing = slot_index * quarter + my_pick
    outgoing = (
        jnp.zeros((front_count * capacity, TILE, TILE), jnp.float32).at[position].set(arrived)
    )
    labels = jnp.zeros((front_count * capacity,), jnp.int32).at[position].set(landing)
    received, received_labels = (
        lax.all_to_all(
            outgoing.reshape(front_count, capacity, TILE, TILE),
            "front",
            split_axis=0,
            concat_axis=0,
            tiled=True,
        ),
        lax.all_to_all(
            labels.reshape(front_count, capacity), "front", split_axis=0, concat_axis=0, tiled=True
        ),
    )
    tile_sums = (
        jnp.zeros((PB * quarter, TILE, TILE), jnp.float32)
        .at[received_labels.reshape(-1)]
        .add(received.reshape(-1, TILE, TILE))
    )
    panel_update = (
        tile_sums.reshape(PB, quarter, TILE, TILE)
        .transpose(0, 2, 1, 3)
        .reshape(PB * TILE, quarter * TILE)
    )
    updated = parent_rows - panel_update
    row_major = lax.all_to_all(updated, "blk", split_axis=0, concat_axis=1, tiled=True)
    columns = block_ids * quarter + column_picks
    my_top = lax.dynamic_slice_in_dim(top_solved, my_block * TILE, TILE, 0)
    cross_terms = jnp.dot(my_top, top_solved.T, precision=HIGHEST)
    cross_terms = cross_terms.reshape(TILE, block_count, TILE).transpose(1, 0, 2)
    row_block = my_block * quarter + my_pick
    spread = (
        jnp.zeros((block_width, TILE, block_width, TILE), jnp.float32)
        .at[row_block, :, columns, :]
        .set(cross_terms)
    )
    owner_mask = jnp.where(lax.axis_index("front") == 0, 1.0, 0.0).astype(jnp.float32)
    placed = lax.dynamic_update_slice_in_dim(
        jnp.zeros((W, W), jnp.float32), parent_diag * owner_mask, my_block * quarter * TILE, 0
    )
    whole_diag = lax.psum(placed - spread.reshape(W, W), ("front", "blk"))
    parent_factor = blocked_cholesky(whole_diag)
    own_rows = lax.dynamic_slice_in_dim(parent_factor, my_block * quarter * TILE, quarter * TILE, 0)
    return (own_rows, right_solve(parent_factor, row_major))


def solution(mesh):
    return jax.shard_map(
        shards,
        mesh=mesh,
        in_specs=(
            P(("front", "blk"), None),
            P(("front", "blk"), None),
            P(("front", "blk"), None),
            P("front", None, None),
            P("front", None),
            P("front", None),
            P("blk", None),
            P("front", "blk"),
        ),
        out_specs=(P("blk", None), P(("front", "blk"), None)),
        check_vma=False,
    )
```

profile of v0, /device:TPU:2, one launch (start us, length us, event | category | flops | bytes accessed | tf_op | source)
XLA Modules:
  0.0 1292.2 jit_solution(12158726002848538924)
XLA Ops:
  12.9 81.6 %all-gather.3.cloned.1.call-done = f32[1024,1024]{0,1:T(8,128)} async-done(((f32[256,1024]{0,1:T(8,128)}), f32[1024,1024]{0,1:T(8,128)}) %all-gather.3.cloned.1.call-update) | async-done | bytes 4194320 | tf_op jit(solution)/shard_map/all_gather | solution.py:46
  96.6 11.7 cholesky.382
  108.4 9.8 custom-call.38
  118.7 11.7 cholesky.399
  136.4 20.1 %custom-call.39 = f32[2,128,128]{1,2,0:T(8,128)S(1)} custom-call(f32[2,128,128]{2,1,0:T(8,128)S(1)} %get-tuple-element.311), custom_call_target="InvertDiagBlocksLowerTriangular" | custom-call | tf_op jit(solution)/shard_map/jit(_solve_triangular)/triangular_solve | solution.py:14
  169.0 11.7 cholesky.416
  180.8 10.4 custom-call.40
  192.5 11.9 cholesky.433
  212.0 19.7 %custom-call.41 = f32[2,128,128]{1,2,0:T(8,128)S(1)} custom-call(f32[2,128,128]{2,1,0:T(8,128)S(1)} %get-tuple-element.312), custom_call_target="InvertDiagBlocksLowerTriangular" | custom-call | tf_op jit(solution)/shard_map/jit(_solve_triangular)/triangular_solve | solution.py:14
  238.9 11.7 cholesky.450
  250.6 9.8 custom-call.42
  260.9 11.7 cholesky.467
  280.3 20.1 %custom-call.43 = f32[2,128,128]{1,2,0:T(8,128)S(1)} custom-call(f32[2,128,128]{2,1,0:T(8,128)S(1)} %get-tuple-element.313), custom_call_target="InvertDiagBlocksLowerTriangular" | custom-call | tf_op jit(solution)/shard_map/jit(_solve_triangular)/triangular_solve | solution.py:14
  302.0 11.7 cholesky.484
  313.8 9.8 custom-call.44
  324.1 11.7 cholesky.501
  340.1 4.8 fusion.1
  344.9 23.0 %while.41 = (s32[]{:T(128)}, f32[1024,1024]{1,0:T(8,128)}, s32[8,2]{0,1:T(2,128)S(1)}, f32[8,128,128]{2,1,0:T(8,128)S(1)}, s32[]{:T(128)}) while((s32[]{:T(128)}, f32[1024,1024]{1,0:T(8,128)}, s32[8,2]{0,1:T(2,128)S(1)}, f32[8,128,128]{2,1,0:T(8,128)S(1)}, s32[]{:T(128)}) %tuple.338), condition=%wide.while_cond.23, body=%wide.while_body.23.sunk | while | flops 2 | bytes 131181 | solution.py:14
  367.9 78.8 %custom-call.45 = f32[8,128,128]{1,2,0:T(8,128)S(1)} custom-call(f32[8,128,128]{2,1,0:T(8,128)S(1)} %get-tuple-element.314), custom_call_target="InvertDiagBlocksLowerTriangular" | custom-call | tf_op jit(solution)/shard_map/jit(_solve_triangular)/triangular_solve | solution.py:14
  487.1 6.7 fusion.4
  493.8 9.4 all-to-all-start.1
  512.9 16.0 %all-to-all-done.1 = f32[4,512,128]{1,2,0:T(8,128)S(1)} async-done(((f32[4,512,128]{1,2,0:T(8,128)}), f32[4,512,128]{1,2,0:T(8,128)S(1)}, u32[]{:S(2)}, u32[]{:S(2)}) %all-to-all-start.1) | async-done | bytes 1048608 | tf_op jit(solution)/shard_map/all_to_all | solution.py:54
  528.9 10.3 all-to-all-start
  540.6 4.3 broadcast_in_dim.27
  547.8 9.0 all-to-all-start.2
  563.1 5.5 copy.213
  568.6 7.0 bitcast_subtract_fusion
  577.0 314.4 %all-reduce.6.cloned.1.call-done = f32[1024,1024]{0,1:T(8,128)} async-done(((f32[1024,1024]{0,1:T(8,128)}), f32[1024,1024]{0,1:T(8,128)}) %all-reduce.6.cloned.1.call-update) | async-done | bytes 4194320 | tf_op jit(solution)/shard_map/psum | solution.py:108
  893.4 11.7 cholesky.518
  905.3 9.8 custom-call.46
  915.7 11.7 cholesky.535
  935.4 19.7 %custom-call.47 = f32[2,128,128]{1,2,0:T(8,128)S(1)} custom-call(f32[2,128,128]{2,1,0:T(8,128)S(1)} %get-tuple-element.315), custom_call_target="InvertDiagBlocksLowerTriangular" | custom-call | tf_op jit(solution)/shard_map/jit(_solve_triangular)/triangular_solve | solution.py:14
  962.9 11.7 cholesky.552
  974.7 9.8 custom-call.48
  986.8 11.9 cholesky.569
  1010.9 19.7 %custom-call.49 = f32[2,128,128]{1,2,0:T(8,128)S(1)} custom-call(f32[2,128,128]{2,1,0:T(8,128)S(1)} %get-tuple-element.316), custom_call_target="InvertDiagBlocksLowerTriangular" | custom-call | tf_op jit(solution)/shard_map/jit(_solve_triangular)/triangular_solve | solution.py:14
  1033.3 11.7 cholesky.586
  1045.1 9.8 custom-call.50
  1055.5 12.1 cholesky.603
  1076.4 19.7 %custom-call.51 = f32[2,128,128]{1,2,0:T(8,128)S(1)} custom-call(f32[2,128,128]{2,1,0:T(8,128)S(1)} %get-tuple-element.317), custom_call_target="InvertDiagBlocksLowerTriangular" | custom-call | tf_op jit(solution)/shard_map/jit(_solve_triangular)/triangular_solve | solution.py:14
  1097.8 11.7 cholesky.620
  1109.6 9.8 custom-call.52
  1120.0 11.7 cholesky.637
  1136.0 4.7 fusion
  1140.8 17.2 %scatter_fusion.2 = f32[8,128,128]{2,1,0:T(8,128)S(1)} fusion(f32[8,128,128]{2,1,0:T(8,128)S(1)} %broadcast.606.clone.1, s32[128]{0:T(128)S(1)} %fusion.185, f32[128,128,128]{2,1,0:T(8,128)} %bitcast.84), kind=kCustom, calls=%fused_computation.3 | custom fusion | flops 2097152 | bytes 25166336 | tf_op jit(solution)/shard_map/scatter-add | solution.py:85
  1159.3 5.6 all-to-all-start.3
  1164.9 25.1 %while.37 = (s32[]{:T(128)}, f32[1024,1024]{0,1:T(8,128)}, s32[8,2]{0,1:T(2,128)S(1)}, f32[8,128,128]{2,1,0:T(8,128)S(1)}, s32[]{:T(128)}) while((s32[]{:T(128)}, f32[1024,1024]{0,1:T(8,128)}, s32[8,2]{0,1:T(2,128)S(1)}, f32[8,128,128]{2,1,0:T(8,128)S(1)}, s32[]{:T(128)}) %tuple.359), condition=%wide.while_cond.24, body=%wide.while_body.24.sunk | while | flops 2 | bytes 393321 | solution.py:14
  1189.9 78.6 %custom-call.24 = f32[8,128,128]{1,2,0:T(8,128)S(1)} custom-call(f32[8,128,128]{2,1,0:T(8,128)S(1)} %get-tuple-element.286), custom_call_target="InvertDiagBlocksLowerTriangular" | custom-call | tf_op jit(solution)/shard_map/jit(_solve_triangular)/triangular_solve | solution.py:14
  (402 shorter events, 249.5 us)
Async XLA Ops:
  7.2 2.8 copy-start.13
  7.2 3.9 copy-start.9
  7.2 87.3 %all-gather.3.cloned.1.call-start = ((), (), s32[]{:S(2)}) async-start(), calls=%async_computation.4 | async-start | bytes 5242880 | tf_op jit(solution)/shard_map/all_gather | solution.py:46
  9.9 456.9 %all-gather.5.cloned.1.call-start = ((), (), s32[]{:S(2)}) async-start(), calls=%async_computation.5 | async-start | bytes 2621440 | tf_op jit(solution)/shard_map/all_gather | solution.py:47
  234.1 3.7 copy-start.8
  340.1 106.7 %copy-start = (f32[512,1024]{0,1:T(8,128)S(1)}, f32[512,1024]{0,1:T(8,128)}, u32[]{:S(2)}) copy-start(f32[512,1024]{0,1:T(8,128)} %copy.238) | copy-start | bytes 6291460
  466.8 3.4 copy-start.10
  493.8 9.4 copy-start.14
  493.8 10.7 copy-start.16
  493.8 10.9 copy-start.15
  493.8 35.1 %all-to-all-start.1 = ((f32[4,512,128]{1,2,0:T(8,128)}), f32[4,512,128]{1,2,0:T(8,128)S(1)}, u32[]{:S(2)}, u32[]{:S(2)}) async-start(f32[4,512,128]{1,2,0:T(8,128)} %fusion.4), calls=%async_computation.1 | async-start | bytes 2097152 | tf_op jit(solution)/shard_map/all_to_all | solution.py:54
  509.3 2.5 copy-start.4
  528.9 18.9 %all-to-all-start = ((s32[64,1,2]{2,1,0:T(1,128)}), s32[64,1,2]{2,1,0:T(1,128)S(1)}, u32[]{:S(2)}, u32[]{:S(2)}) async-start(s32[64,1,2]{2,1,0:T(1,128)} %bitcast.67), calls=%async_computation | async-start | bytes 65536 | tf_op jit(solution)/shard_map/all_to_all | solution.py:78
  540.6 4.3 copy-start.1
  547.8 592.9 %all-to-all-start.2 = ((f32[64,2,128,128]{3,2,1,0:T(8,128)}), f32[64,2,128,128]{3,2,1,0:T(8,128)}, u32[]{:S(2)}, u32[]{:S(2)}) async-start(f32[64,2,128,128]{3,2,1,0:T(8,128)} %bitcast.457), calls=%async_computation.2 | async-start | bytes 16777216 | tf_op jit(solution)/shard_map/all_to_all | solution.py:71
  556.9 334.5 %all-reduce.6.cloned.1.call-start = ((), (), s32[]{:S(2)}) async-start(), calls=%async_computation.6 | async-start | bytes 8388608 | tf_op jit(solution)/shard_map/psum | solution.py:108
  955.1 2.9 copy-start.5
  962.1 0.7 copy-start.11
  1031.0 2.0 copy-start.2
  1031.9 1.1 copy-start.6
  1033.0 37.4 %copy-start.3 = (f32[128,512]{1,0:T(8,128)S(1)}, f32[128,512]{1,0:T(8,128)}, u32[]{:S(2)}) copy-start(f32[128,512]{1,0:T(8,128)} %copy-done.2) | copy-start | bytes 786436
  1033.1 37.4 %copy-start.7 = (f32[128,512]{1,0:T(8,128)S(1)}, f32[128,512]{1,0:T(8,128)}, u32[]{:S(2)}) copy-start(f32[128,512]{1,0:T(8,128)} %copy-done.6) | copy-start | bytes 786436
  1140.8 17.6 %copy-start.12 = (f32[512,256]{1,0:T(8,128)S(1)}, f32[512,256]{1,0:T(8,128)}, u32[]{:S(2)}) copy-start(f32[512,256]{1,0:T(8,128)} %param.64) | copy-start | bytes 1572868
  1159.3 111.9 %all-to-all-start.3 = ((f32[4,128,256]{2,1,0:T(8,128)}), f32[4,128,256]{2,1,0:T(8,128)S(1)}, u32[]{:S(2)}, u32[]{:S(2)}) async-start(f32[4,128,256]{2,1,0:T(8,128)} %bitcast.87), calls=%async_computation.3 | async-start | bytes 1048576 | tf_op jit(solution)/shard_map/all_to_all | solution.py:93
Sparse Core Ops, SparseCore 0:
  10.4 84.0 all-gather.2
  96.9 59.9 all-gather.4
  575.7 315.6 all-reduce.5
where the time goes:
time: 1300 us; the launch traced here: 1290 us
  other arithmetic  605 us (47%)
  waiting for transfers between devices  412 us (32%)
  local copies, waits for them, and re-layouts  128 us (10%)
  matrix products  85.6 us (7%)
  starting transfers between devices  34.5 us (3%)
  between operations  26.6 us (2%)
    psum x1, waiting for transfers between devices, shards(): whole_diag = lax.psum(placed - spread.reshape(W, W), ('front', 'blk'))  314 us
    another operation x18, other arithmetic, right_solve(): return jax.scipy.linalg.solve_triangular(factor, matrix.T, lower=True).T  290 us
    another operation x55, other arithmetic, blocked_cholesky(): diag_piece = jnp.linalg.cholesky(remaining[offset:finish, offset:finish])  278 us
    all_gather x1, waiting for transfers between devices, shards(): lax.all_gather(child_diag, 'blk', axis=0, tiled=True)  81.6 us
    another operation x63, matrix products, right_solve(): return jax.scipy.linalg.solve_triangular(factor, matrix.T, lower=True).T  61 us
    another operation x86, local copies, waits for them, and re-layouts, right_solve(): return jax.scipy.linalg.solve_triangular(factor, matrix.T, lower=True).T  48.4 us
    another operation x41, local copies, waits for them, and re-layouts  27.3 us
  transfers between devices with their start and end apart: 7, of which 3 were waited for; matrix products, arithmetic and copies ran while one was open for 58% of the time, Pallas kernels for 0%

commit v1 on v0

--- a/solution.py
+++ b/solution.py
@@ -43,7 +43,9 @@
     block_width = W // TILE
     capacity = max(2, 8 * TA // front_count)
     diag_whole, top_whole = (
-        lax.all_gather(child_diag, "blk", axis=0, tiled=True),
+        jnp.concatenate(
+            lax.all_to_all(jnp.stack([child_diag] * lax.axis_size("blk")), "blk", 0, 0), axis=0
+        ),
         lax.all_gather(child_top, "blk", axis=0, tiled=True),
     )
     factor = blocked_cholesky(diag_whole)

time: 1300 us -> 1370 us (1.054)
  waiting for transfers between devices: 412 us -> 455 us
    all_to_all x0 -> x1, waiting for transfers between devices: none -> 127 us  [shards(): lax.all_to_all(jnp.stack([child_diag] * lax.axis_size('blk')), 'blk', 0, 0)]
    all_gather x1 -> x0, waiting for transfers between devices: 81.6 us -> none  [shards(): lax.all_gather(child_diag, 'blk', axis=0, tiled=True)]
    another operation x41 -> x42, local copies, waits for them, and re-layouts: 27.3 us -> 29.6 us
  transfers between devices with their start and end apart: 7 -> 7, of which waited for: 3 -> 3; matrix products, arithmetic and copies ran while one was open for 58% -> 57% of each run, Pallas kernels for 0% -> 0%
where the time goes in v1:
time: 1370 us; the launch traced here: 1350 us
  other arithmetic  618 us (45%)
  waiting for transfers between devices  455 us (33%)
  local copies, waits for them, and re-layouts  132 us (10%)
  matrix products  85.3 us (6%)
  starting transfers between devices  35.8 us (3%)
  between operations  27 us (2%)
    psum x1, waiting for transfers between devices, shards(): whole_diag = lax.psum(placed - spread.reshape(W, W), ('front', 'blk'))  314 us
    another operation x18, other arithmetic, right_solve(): return jax.scipy.linalg.solve_triangular(factor, matrix.T, lower=True).T  303 us
    another operation x55, other arithmetic, blocked_cholesky(): diag_piece = jnp.linalg.cholesky(remaining[offset:finish, offset:finish])  278 us
    all_to_all x1, waiting for transfers between devices, shards(): lax.all_to_all(jnp.stack([child_diag] * lax.axis_size('blk')), 'blk', 0, 0)  127 us
    another operation x63, matrix products, right_solve(): return jax.scipy.linalg.solve_triangular(factor, matrix.T, lower=True).T  60.7 us
    another operation x86, local copies, waits for them, and re-layouts, right_solve(): return jax.scipy.linalg.solve_triangular(factor, matrix.T, lower=True).T  48.4 us
  transfers between devices with their start and end apart: 7, of which 3 were waited for; matrix products, arithmetic and copies ran while one was open for 57% of the time, Pallas kernels for 0%

profile of v1, /device:TPU:2, one launch (start us, length us, event | category | flops | bytes accessed | tf_op | source)
XLA Modules:
  0.0 1353.3 jit_solution(10305692180092666966)
XLA Ops:
  11.0 8.7 all-to-all-start
  22.6 126.7 %all-to-all-done = f32[4,256,1024]{1,2,0:T(8,128)} async-done(((f32[4,256,1024]{1,2,0:T(8,128)}), f32[4,256,1024]{1,2,0:T(8,128)}, u32[]{:S(2)}, u32[]{:S(2)}) %all-to-all-start) | async-done | bytes 4194336 | tf_op jit(solution)/shard_map/all_to_all | solution.py:47
  155.3 11.7 cholesky.382
  167.0 9.8 custom-call.38
  177.3 11.7 cholesky.399
  195.0 32.9 %custom-call.39 = f32[2,128,128]{1,2,0:T(8,128)S(1)} custom-call(f32[2,128,128]{2,1,0:T(8,128)S(1)} %get-tuple-element.311), custom_call_target="InvertDiagBlocksLowerTriangular" | custom-call | tf_op jit(solution)/shard_map/jit(_solve_triangular)/triangular_solve | solution.py:14
  239.2 11.7 cholesky.416
  250.9 10.4 custom-call.40
  262.7 11.7 cholesky.433
  282.0 20.1 %custom-call.41 = f32[2,128,128]{1,2,0:T(8,128)S(1)} custom-call(f32[2,128,128]{2,1,0:T(8,128)S(1)} %get-tuple-element.312), custom_call_target="InvertDiagBlocksLowerTriangular" | custom-call | tf_op jit(solution)/shard_map/jit(_solve_triangular)/triangular_solve | solution.py:14
  309.3 11.7 cholesky.450
  321.0 9.8 custom-call.42
  331.3 11.7 cholesky.467
  350.7 19.9 %custom-call.43 = f32[2,128,128]{1,2,0:T(8,128)S(1)} custom-call(f32[2,128,128]{2,1,0:T(8,128)S(1)} %get-tuple-element.313), custom_call_target="InvertDiagBlocksLowerTriangular" | custom-call | tf_op jit(solution)/shard_map/jit(_solve_triangular)/triangular_solve | solution.py:14
  372.2 11.7 cholesky.484
  384.0 9.8 custom-call.44
  394.3 11.7 cholesky.501
  410.2 4.8 fusion.1
  415.1 23.0 %while.41 = (s32[]{:T(128)}, f32[1024,1024]{1,0:T(8,128)}, s32[8,2]{0,1:T(2,128)S(1)}, f32[8,128,128]{2,1,0:T(8,128)S(1)}, s32[]{:T(128)}) while((s32[]{:T(128)}, f32[1024,1024]{1,0:T(8,128)}, s32[8,2]{0,1:T(2,128)S(1)}, f32[8,128,128]{2,1,0:T(8,128)S(1)}, s32[]{:T(128)}) %tuple.338), condition=%wide.while_cond.23, body=%wide.while_body.23.sunk | while | flops 2 | bytes 131181 | solution.py:14
  438.1 79.0 %custom-call.45 = f32[8,128,128]{1,2,0:T(8,128)S(1)} custom-call(f32[8,128,128]{2,1,0:T(8,128)S(1)} %get-tuple-element.314), custom_call_target="InvertDiagBlocksLowerTriangular" | custom-call | tf_op jit(solution)/shard_map/jit(_solve_triangular)/triangular_solve | solution.py:14
  557.3 6.7 fusion.4
  577.4 13.5 all-to-all-done.2
  590.8 8.8 all-to-all-start.1
  601.0 4.3 broadcast_in_dim.27
  608.2 9.0 all-to-all-start.3
  623.5 5.7 copy.215
  629.2 7.0 bitcast_subtract_fusion
  637.6 314.5 %all-reduce.6.cloned.1.call-done = f32[1024,1024]{0,1:T(8,128)} async-done(((f32[1024,1024]{0,1:T(8,128)}), f32[1024,1024]{0,1:T(8,128)}) %all-reduce.6.cloned.1.call-update) | async-done | bytes 4194320 | tf_op jit(solution)/shard_map/psum | solution.py:110
  954.2 11.7 cholesky.518
  966.0 9.8 custom-call.46
  976.4 11.7 cholesky.535
  995.9 19.7 %custom-call.47 = f32[2,128,128]{1,2,0:T(8,128)S(1)} custom-call(f32[2,128,128]{2,1,0:T(8,128)S(1)} %get-tuple-element.315), custom_call_target="InvertDiagBlocksLowerTriangular" | custom-call | tf_op jit(solution)/shard_map/jit(_solve_triangular)/triangular_solve | solution.py:14
  1023.4 11.7 cholesky.552
  1035.2 9.8 custom-call.48
  1047.3 12.1 cholesky.569
  1071.6 19.7 %custom-call.49 = f32[2,128,128]{1,2,0:T(8,128)S(1)} custom-call(f32[2,128,128]{2,1,0:T(8,128)S(1)} %get-tuple-element.316), custom_call_target="InvertDiagBlocksLowerTriangular" | custom-call | tf_op jit(solution)/shard_map/jit(_solve_triangular)/triangular_solve | solution.py:14
  1094.0 11.7 cholesky.586
  1105.8 9.8 custom-call.50
  1116.2 11.9 cholesky.603
  1136.8 19.7 %custom-call.51 = f32[2,128,128]{1,2,0:T(8,128)S(1)} custom-call(f32[2,128,128]{2,1,0:T(8,128)S(1)} %get-tuple-element.317), custom_call_target="InvertDiagBlocksLowerTriangular" | custom-call | tf_op jit(solution)/shard_map/jit(_solve_triangular)/triangular_solve | solution.py:14
  1158.3 11.7 cholesky.620
  1170.1 9.8 custom-call.52
  1180.5 11.7 cholesky.637
  1196.5 4.7 fusion
  1201.3 17.2 %scatter_fusion.2 = f32[8,128,128]{2,1,0:T(8,128)S(1)} fusion(f32[8,128,128]{2,1,0:T(8,128)S(1)} %broadcast.608.clone.1, s32[128]{0:T(128)S(1)} %fusion.185, f32[128,128,128]{2,1,0:T(8,128)} %bitcast.84), kind=kCustom, calls=%fused_computation.3 | custom fusion | flops 2097152 | bytes 25166336 | tf_op jit(solution)/shard_map/scatter-add | solution.py:87
  1219.8 5.6 all-to-all-start.4
  1225.4 25.1 %while.37 = (s32[]{:T(128)}, f32[1024,1024]{0,1:T(8,128)}, s32[8,2]{0,1:T(2,128)S(1)}, f32[8,128,128]{2,1,0:T(8,128)S(1)}, s32[]{:T(128)}) while((s32[]{:T(128)}, f32[1024,1024]{0,1:T(8,128)}, s32[8,2]{0,1:T(2,128)S(1)}, f32[8,128,128]{2,1,0:T(8,128)S(1)}, s32[]{:T(128)}) %tuple.357), condition=%wide.while_cond.24, body=%wide.while_body.24.sunk | while | flops 2 | bytes 393321 | solution.py:14
  1250.5 78.6 %custom-call.24 = f32[8,128,128]{1,2,0:T(8,128)S(1)} custom-call(f32[8,128,128]{2,1,0:T(8,128)S(1)} %get-tuple-element.286), custom_call_target="InvertDiagBlocksLowerTriangular" | custom-call | tf_op jit(solution)/shard_map/jit(_solve_triangular)/triangular_solve | solution.py:14
  (405 shorter events, 256.3 us)
Async XLA Ops:
  11.0 8.7 copy-start.14
  11.0 9.8 copy-start.10
  11.0 138.3 %all-to-all-start = ((f32[4,256,1024]{1,2,0:T(8,128)}), f32[4,256,1024]{1,2,0:T(8,128)}, u32[]{:S(2)}, u32[]{:S(2)}) async-start(f32[4,256,1024]{1,2,0:T(8,128)} %stack.2), calls=%async_computation | async-start | bytes 8388608 | tf_op jit(solution)/shard_map/all_to_all | solution.py:47
  19.8 517.5 %all-gather.2.cloned.1.call-start = ((), (), s32[]{:S(2)}) async-start(), calls=%async_computation.5 | async-start | bytes 2621440 | tf_op jit(solution)/shard_map/all_gather | solution.py:49
  152.1 1.9 copy-start
  304.5 3.7 copy-start.9
  410.2 106.9 %copy-start.1 = (f32[512,1024]{0,1:T(8,128)S(1)}, f32[512,1024]{0,1:T(8,128)}, u32[]{:S(2)}) copy-start(f32[512,1024]{0,1:T(8,128)} %copy.240) | copy-start | bytes 6291460
  537.2 3.4 copy-start.11
  564.0 3.7 copy-start.15
  564.0 5.0 copy-start.17
  564.0 5.2 copy-start.16
  564.0 26.8 %all-to-all-start.2 = ((f32[4,512,128]{1,2,0:T(8,128)}), f32[4,512,128]{1,2,0:T(8,128)S(1)}, u32[]{:S(2)}, u32[]{:S(2)}) async-start(f32[4,512,128]{1,2,0:T(8,128)} %fusion.4), calls=%async_computation.2 | async-start | bytes 2097152 | tf_op jit(solution)/shard_map/all_to_all | solution.py:56
  573.8 2.5 copy-start.5
  590.8 17.4 %all-to-all-start.1 = ((s32[64,1,2]{2,1,0:T(1,128)}), s32[64,1,2]{2,1,0:T(1,128)S(1)}, u32[]{:S(2)}, u32[]{:S(2)}) async-start(s32[64,1,2]{2,1,0:T(1,128)} %bitcast.67), calls=%async_computation.1 | async-start | bytes 65536 | tf_op jit(solution)/shard_map/all_to_all | solution.py:80
  601.0 4.3 copy-start.2
  608.2 593.0 %all-to-all-start.3 = ((f32[64,2,128,128]{3,2,1,0:T(8,128)}), f32[64,2,128,128]{3,2,1,0:T(8,128)}, u32[]{:S(2)}, u32[]{:S(2)}) async-start(f32[64,2,128,128]{3,2,1,0:T(8,128)} %bitcast.459), calls=%async_computation.3 | async-start | bytes 16777216 | tf_op jit(solution)/shard_map/all_to_all | solution.py:73
  617.3 334.8 %all-reduce.6.cloned.1.call-start = ((), (), s32[]{:S(2)}) async-start(), calls=%async_computation.6 | async-start | bytes 8388608 | tf_op jit(solution)/shard_map/psum | solution.py:110
  1015.6 2.9 copy-start.6
  1022.6 0.7 copy-start.12
  1091.8 2.0 copy-start.3
  1092.6 1.1 copy-start.7
  1093.8 37.1 %copy-start.4 = (f32[128,512]{1,0:T(8,128)S(1)}, f32[128,512]{1,0:T(8,128)}, u32[]{:S(2)}) copy-start(f32[128,512]{1,0:T(8,128)} %copy-done.3) | copy-start | bytes 786436
  1093.8 37.1 %copy-start.8 = (f32[128,512]{1,0:T(8,128)S(1)}, f32[128,512]{1,0:T(8,128)}, u32[]{:S(2)}) copy-start(f32[128,512]{1,0:T(8,128)} %copy-done.7) | copy-start | bytes 786436
  1201.3 17.7 %copy-start.13 = (f32[512,256]{1,0:T(8,128)S(1)}, f32[512,256]{1,0:T(8,128)}, u32[]{:S(2)}) copy-start(f32[512,256]{1,0:T(8,128)} %param.64) | copy-start | bytes 1572868
  1219.8 111.9 %all-to-all-start.4 = ((f32[4,128,256]{2,1,0:T(8,128)}), f32[4,128,256]{2,1,0:T(8,128)S(1)}, u32[]{:S(2)}, u32[]{:S(2)}) async-start(f32[4,128,256]{2,1,0:T(8,128)} %bitcast.87), calls=%async_computation.4 | async-start | bytes 1048576 | tf_op jit(solution)/shard_map/all_to_all | solution.py:95
Sparse Core Ops, SparseCore 0:
  23.0 118.3 all-gather.1
  636.3 315.6 all-reduce.5
